TPU v7x, 32 devices: a whole 2x2x4 slice. The times are simulated.
32 devices in a mesh: expert: 8 (over z, x), tensor: 4 (over y, core).
Axes of the slice: x: 2, y: 2, z: 4, core: 2. Of those that a mesh axis runs over, the one named last changes fastest.
Arguments:
- tokens: bfloat16 [512, 1536], P('expert'), may hold values from -6 to 6
- exponents: int32 [512, 12], P('expert'), may hold values from -1 to 1
- out_grad: bfloat16 [512, 1536], P('expert'), may hold values from -6 to 6
- slots: int32 [8, 128], replicated, may hold values from 0 to 511, as said below
- gates: float32 [8, 128], P('expert'), may hold values from 0.1 to 1
- w_in: bfloat16 [8, 1536, 4096], P('expert', None, 'tensor'), may hold values from -0.15625 to 0.15625
- w_out: bfloat16 [8, 4096, 1536], P('expert', 'tensor'), may hold values from -0.09375 to 0.09375
Outputs:
- token_grad: bfloat16 [512, 1536], P(('expert', 'tensor'))
- w_in_grad: bfloat16 [8, 1536, 4096], P('expert', None, 'tensor')
- w_out_grad: bfloat16 [8, 4096, 1536], P('expert', 'tensor')
- gate_grad: float32 [8, 128], P('expert')
Inputs may be any that keep to these rules, and one draw needn't show every extreme that they name: `slots`: each row holds 128 distinct token indices. In every row, at most 20 indices fall in any aligned block of 64 tokens (the tokens of one index of expert), and some block holds exactly 20.
All inputs are finite; a program needn't handle non-finite values.
Results may differ from a plain program's by a relative error of at most 0.007.
Values may be sent and summed in bfloat16 or wider, within the bound.
A program may use at most 64 MiB of HBM per device.

v0:
```python
import functools
import math

import jax
import jax.numpy as jnp
from jax import lax
from jax.experimental import pallas as pl
from jax.experimental.pallas import tpu as pltpu
from jax.sharding import PartitionSpec as P

MESH = pl.DeviceIdType.MESH
ROOT = math.sqrt(2.0 / math.pi)
CUBIC = 0.044715


def contract(left, right, left_dim, right_dim):
    return lax.dot_general(
        left, right, (((left_dim,), (right_dim,)), ((), ())), preferred_element_type=jnp.float32
    )


def apply_scales(values, exponents):
    row_count = values.shape[0]
    block_count = exponents.shape[1]
    factors = jnp.exp2(exponents.astype(jnp.float32))
    widened = values.astype(jnp.float32).reshape(row_count, block_count, 128) * factors[:, :, None]
    return widened.reshape(row_count, block_count * 128)


def local(tokens, exponents, out_grad, slots, gates, w_in, w_out):
    expert_count = lax.axis_size("expert")
    my_expert = lax.axis_index("expert")
    my_tensor = lax.axis_index("tensor")
    tok_count = tokens.shape[0]
    model_width = tokens.shape[1]
    slot_count = slots.shape[1]
    capacity = slot_count // expert_count + slot_count // (4 * expert_count)
    total_slots = expert_count * capacity
    owner = slots // tok_count
    local_index = slots % tok_count
    from_here = owner == my_expert
    send_order = jnp.cumsum(from_here.astype(jnp.int32), axis=1) - 1
    rank_range = jnp.arange(capacity, dtype=jnp.int32)
    send_hit = from_here[:, :, None] & (send_order[:, :, None] == rank_range[None, None, :])
    send_valid = jnp.any(send_hit, axis=1)
    picked_index = jnp.sum(jnp.where(send_hit, local_index[:, :, None], 0), axis=1)
    send_table = jnp.where(send_valid, picked_index, tok_count)
    row_owner = lax.dynamic_index_in_dim(owner, my_expert, 0, keepdims=False)
    slot_range = jnp.arange(slot_count, dtype=jnp.int32)
    earlier = (row_owner[:, None] == row_owner[None, :]) & (
        slot_range[:, None] > slot_range[None, :]
    )
    row_rank = jnp.sum(earlier.astype(jnp.int32), axis=1)
    flat_index = row_owner * capacity + row_rank
    scaled_local = apply_scales(tokens, exponents).astype(jnp.bfloat16)
    sent_rows = jnp.take(scaled_local, send_table, axis=0, mode="fill", fill_value=0)
    sent_grads = jnp.take(out_grad, send_table, axis=0, mode="fill", fill_value=0)
    arrived_rows, arrived_grads = (
        lax.all_to_all(sent_rows, "expert", split_axis=0, concat_axis=0, tiled=True),
        lax.all_to_all(sent_grads, "expert", split_axis=0, concat_axis=0, tiled=True),
    )
    slot_rows = arrived_rows.reshape(total_slots, model_width)
    slot_grads = arrived_grads.reshape(total_slots, model_width)
    gate_row = jnp.zeros((total_slots,), jnp.float32).at[flat_index].set(gates[0])
    weight_in = w_in[0]
    weight_out = w_out[0]
    preact = jnp.dot(slot_rows, weight_in, preferred_element_type=jnp.float32)
    hidden_full, backward = jax.vjp(jax.nn.gelu, preact)
    hidden = hidden_full.astype(jnp.bfloat16)
    upstream = contract(slot_grads, weight_out, 1, 1)
    gate_part = jnp.sum(hidden.astype(jnp.float32) * upstream, axis=1)
    gate_total = lax.psum(gate_part[flat_index], "tensor")
    dpre = backward(gate_row[:, None] * upstream)[0].astype(jnp.bfloat16)
    gated_grads = (gate_row[:, None] * slot_grads.astype(jnp.float32)).astype(jnp.bfloat16)
    out_weight_grad = contract(hidden, gated_grads, 0, 0).astype(jnp.bfloat16)
    in_weight_grad = contract(slot_rows, dpre, 0, 0).astype(jnp.bfloat16)
    slot_back = contract(dpre, weight_in, 1, 1)
    flat_send = send_table.reshape(-1)
    came_back = lax.all_to_all(
        slot_back.reshape(expert_count, capacity, model_width),
        "expert",
        split_axis=0,
        concat_axis=0,
        tiled=True,
    )
    token_sums = (
        jnp.zeros((tok_count, model_width), jnp.float32)
        .at[flat_send]
        .add(came_back.reshape(total_slots, model_width), mode="drop")
    )
    my_share = lax.psum_scatter(token_sums, "tensor", scatter_dimension=0, tiled=True)
    share_rows = my_share.shape[0]
    my_scales = lax.dynamic_slice_in_dim(exponents, my_tensor * share_rows, share_rows, 0)
    token_grad = apply_scales(my_share, my_scales).astype(jnp.bfloat16)
    return (token_grad, in_weight_grad[None], out_weight_grad[None], gate_total[None])


def message(picks, extra_picks, rows):
    third = rows.shape[1] // 3
    lead = jnp.dot(picks, rows, preferred_element_type=jnp.float32)
    rest = sum(
        jnp.dot(extra_picks[c], rows[:, c * third : (c + 1) * third], preferred_element_type=jnp.float32)
        for c in range(3)
    )
    return jnp.concatenate([lead, rest], axis=1).astype(jnp.bfloat16)


def exchange_kernel(
    experts, tensors,
    tokens_hbm, exponents_hbm, out_grad_hbm, slots_hbm, gates_hbm, w_in_hbm, w_out_hbm,
    token_out, gate_out, rows_out, gated_out, hidden_out, dpre_out,
    token_held, gate_held, rows, gated, hidden, dpre,
    tokens, exponents, out_grad, slots, gates,
    w_in, w_out, scaled, picks, extra_picks, place, outgoing, parts, grads, preact,
    core_out, core_in, side_out, side_in, mine, back_out, back_in, last_out, last_in, gate_parts,
    load_sem, send_sem, recv_sem, pass_send, pass_recv, ret_send, ret_recv, side_send, side_recv,
    back_send, back_recv, last_send, last_recv, gate_send, gate_recv, store_sem,
):
    me = lax.axis_index("expert")
    t = lax.axis_index("tensor")
    y, core = t // 2, t % 2
    buddy = 2 * y + (1 - core)
    across = 2 * (1 - y) + core
    diagonal = 2 * (1 - y) + (1 - core)
    tok_count, width = tokens.shape
    quarter = width // tensors
    third = quarter // 3
    capacity = slots.shape[1]
    lead_rows = experts * 16

    loads = [
        pltpu.make_async_copy(source, held, load_sem.at[i])
        for i, (source, held) in enumerate(
            (
                (slots_hbm, slots), (exponents_hbm, exponents), (tokens_hbm, tokens), (out_grad_hbm, out_grad),
                (gates_hbm, gates), (w_in_hbm, w_in), (w_out_hbm, w_out),
            )
        )
    ]
    for load in loads:
        load.start()

    barrier = pltpu.get_barrier_semaphore()
    z, x = me // 2, me % 2
    order = [(z + 2) % 4, 3 - z, z + 1 - 2 * (z % 2), z]
    partner = 2 * z + 1 - x
    peers = [2 * g + i for g in order[:3] for i in (x, 1 - x)] + [partner]
    mates = [buddy, across, diagonal]
    for d in peers:
        pl.semaphore_signal(barrier, inc=1, device_id=(d, t), device_id_type=MESH)
    for m in mates:
        pl.semaphore_signal(barrier, inc=1, device_id=(me, m), device_id_type=MESH)

    tri = (
        lax.broadcasted_iota(jnp.int32, (capacity, capacity), 0)
        < lax.broadcasted_iota(jnp.int32, (capacity, capacity), 1)
    ).astype(jnp.bfloat16)

    def ranks(mask):
        ones = jnp.where(mask, 1.0, 0.0)
        before = jnp.dot(ones.astype(jnp.bfloat16), tri, preferred_element_type=jnp.float32)
        return jnp.where(mask, before, -1.0)

    loads[0].wait()
    all_slots = slots[...]
    local_index = all_slots - me * tok_count
    rank = ranks((local_index >= 0) & (local_index < tok_count))
    local_number = local_index.astype(jnp.float32) + 1.0
    row_id = lax.broadcasted_iota(jnp.int32, (16, capacity), 0)
    lead_target = row_id.astype(jnp.float32)
    rest_target = (16 + row_id % 4).astype(jnp.float32)
    token_id = lax.broadcasted_iota(jnp.int32, (16, tok_count), 1).astype(jnp.float32) + 1.0
    part_id = lax.broadcasted_iota(jnp.int32, (16, tok_count), 0) // 4
    for d in range(experts):
        row_rank, row_number = rank[d : d + 1, :], local_number[d : d + 1, :]
        lead = jnp.sum(jnp.where(row_rank == lead_target, row_number, 0.0), axis=1, keepdims=True)
        rest = jnp.sum(jnp.where(row_rank == rest_target, row_number, 0.0), axis=1, keepdims=True)
        span = pl.ds(d * 16, 16)
        picks[span, :] = jnp.where(lead == token_id, 1.0, 0.0).astype(jnp.bfloat16)
        rest_hit = jnp.where(rest == token_id, 1.0, 0.0)
        for c in range(3):
            extra_picks[c, span, :] = jnp.where(part_id == c, rest_hit, 0.0).astype(jnp.bfloat16)

    blocks = exponents.shape[0]
    eye = (
        lax.broadcasted_iota(jnp.int32, (blocks, blocks), 0) == lax.broadcasted_iota(jnp.int32, (blocks, blocks), 1)
    ).astype(jnp.bfloat16)
    loads[1].wait()
    factors = contract(jnp.exp2(exponents[...].astype(jnp.float32)).astype(jnp.bfloat16), eye, 0, 0)
    loads[2].wait()
    for b in range(width // 128):
        cols = pl.ds(b * 128, 128)
        scaled[:, cols] = (tokens[:, cols].astype(jnp.float32) * factors[:, b : b + 1]).astype(jnp.bfloat16)

    loads[3].wait()
    my_cols = pl.ds(pl.multiple_of(t * quarter, 128), quarter)
    for a, source in enumerate((scaled, out_grad)):
        filled = message(picks[...], extra_picks[...], source[:, my_cols])
        outgoing[a] = filled.reshape(experts, 16, 4 * third)
    for a in range(2):
        parts[a, t, me] = outgoing[a, me]

    def send(a, d):
        return pltpu.make_async_remote_copy(
            src_ref=outgoing.at[a, d], dst_ref=parts.at[a, t, me],
            send_sem=send_sem.at[a, d], recv_sem=recv_sem.at[a, me],
            device_id=(d, t), device_id_type=MESH,
        )

    def arrival(a, k):
        return pltpu.make_async_remote_copy(
            src_ref=outgoing.at[a, k], dst_ref=parts.at[a, t, k],
            send_sem=send_sem.at[a, k], recv_sem=recv_sem.at[a, k],
            device_id=(k, t), device_id_type=MESH,
        )

    groups = experts // 2

    def passing(a, kind, g):
        which, mate = ((t, buddy), (t, across), (across, buddy))[kind]
        block = parts.at[a, which, pl.ds(2 * g, 2)]
        return pltpu.make_async_remote_copy(
            src_ref=block, dst_ref=block,
            send_sem=pass_send.at[a, kind, g], recv_sem=pass_recv.at[a, kind, g],
            device_id=(me, mate), device_id_type=MESH,
        )

    def passed(a, kind, g):
        which, mate = ((buddy, buddy), (across, across), (diagonal, buddy))[kind]
        block = parts.at[a, which, pl.ds(2 * g, 2)]
        return pltpu.make_async_remote_copy(
            src_ref=block, dst_ref=block,
            send_sem=pass_send.at[a, kind, g], recv_sem=pass_recv.at[a, kind, g],
            device_id=(me, mate), device_id_type=MESH,
        )

    pl.semaphore_wait(barrier, len(peers) + len(mates))
    for a in range(2):
        for d in peers:
            send(a, d).start()

    my_slots = slots[pl.ds(me, 1), :] // tok_count
    owner_id = lax.broadcasted_iota(jnp.int32, (experts, capacity), 0)
    own_rank = ranks(jnp.broadcast_to(my_slots, (experts, capacity)) == owner_id)
    lead4 = 16.0 + lax.broadcasted_iota(jnp.int32, (4, capacity), 0).astype(jnp.float32)
    for k in range(experts):
        row_rank = own_rank[k : k + 1, :]
        place[pl.ds(k * 16, 16), :] = jnp.where(row_rank == lead_target, 1.0, 0.0)
        place[pl.ds(lead_rows + k * 4, 4), :] = jnp.where(row_rank == lead4, 1.0, 0.0)
    loads[4].wait()
    gate_flat = jnp.sum(place[...] * gates[...], axis=1, keepdims=True)

    rest_rows = experts * 4
    j = lax.broadcasted_iota(jnp.int32, (3 * rest_rows, lead_rows), 0)
    m = lax.broadcasted_iota(jnp.int32, (3 * rest_rows, lead_rows), 1)
    jr = j % rest_rows
    unpack = (m == (jr // 4) * 16 + 4 * (j // rest_rows) + jr % 4).astype(jnp.bfloat16)

    hidden_block = w_in.shape[1] // groups

    def block_of(i):
        return pl.ds(pl.multiple_of(i * hidden_block, hidden_block), hidden_block)

    near_first = [order[3], order[2], order[0], order[1]]
    for a in range(2):
        for i, g in enumerate(near_first):
            if i == 0:
                arrival(a, partner).wait_recv()
            else:
                arrival(a, 2 * g).wait_recv()
                arrival(a, 2 * g + 1).wait_recv()
            passing(a, 1, g).start()
            passing(a, 0, g).start()

    def relay(a, g):
        passed(a, 1, g).wait_recv()
        passing(a, 2, g).start()

    def arrange(a, target):
        for g in near_first:
            passed(a, 0, g).wait_recv()
        for g in near_first:
            passed(a, 2, g).wait_recv()
        for q in range(tensors):
            target[pl.ds(0, lead_rows), pl.ds(q * quarter, quarter)] = parts[a, q, :, :, pl.ds(0, quarter)].reshape(
                lead_rows, quarter
            )
            rest = jnp.dot(
                unpack, parts[a, q, :, :, pl.ds(quarter, third)].reshape(lead_rows, third),
                preferred_element_type=jnp.float32,
            ).astype(jnp.bfloat16)
            for c in range(3):
                target[pl.ds(lead_rows, rest_rows), pl.ds(q * quarter + c * third, third)] = rest[
                    c * rest_rows : (c + 1) * rest_rows
                ]

    for g in near_first:
        relay(0, g)
    arrange(0, rows)
    loads[5].wait()
    for i, g in enumerate(near_first):
        cols = pl.ds(i * hidden_block, hidden_block)
        preact[:, cols] = jnp.dot(rows[...], w_in[:, cols], preferred_element_type=jnp.float32)
        relay(1, g)
    arrange(1, grads)
    loads[6].wait()

    def backward(i, total):
        cols = block_of(i)
        v = preact[:, cols]
        upstream = contract(grads[...], w_out[cols, :], 1, 1)
        square = v * v
        tanh = jnp.tanh(ROOT * (v + CUBIC * v * square))
        half = 0.5 * (1.0 + tanh)
        act = (v * half).astype(jnp.bfloat16)
        slope = half + 0.5 * v * (1.0 - tanh * tanh) * (ROOT * (1.0 + 3.0 * CUBIC * square))
        hidden[:, cols] = act
        dpre[:, cols] = (gate_flat * upstream * slope).astype(jnp.bfloat16)
        return total + jnp.sum(act.astype(jnp.float32) * upstream, axis=1, keepdims=True)

    gate_part = lax.fori_loop(0, groups, backward, jnp.zeros((place.shape[0], 1), jnp.float32))

    def slot_back(q):
        return contract(dpre[...], w_in[pl.ds(pl.multiple_of(q * quarter, 128), quarter), :], 1, 1)

    def to_core(i):
        return pltpu.make_async_remote_copy(
            src_ref=core_out.at[i], dst_ref=core_in.at[i], send_sem=ret_send.at[i], recv_sem=ret_recv.at[i],
            device_id=(me, buddy), device_id_type=MESH,
        )

    spans = [pl.ds(lead_rows, rest_rows)] + [pl.ds(pl.multiple_of(32 * g, 32), 32) for g in order]

    def to_side(i):
        return pltpu.make_async_remote_copy(
            src_ref=side_out.at[spans[i]], dst_ref=side_in.at[spans[i]],
            send_sem=side_send.at[i], recv_sem=side_recv.at[i],
            device_id=(me, across), device_id_type=MESH,
        )

    core_out[0] = slot_back(diagonal).astype(jnp.bfloat16)
    to_core(0).start()
    partial = slot_back(across)
    to_core(0).wait_recv()
    side_out[...] = (partial + core_in[0].astype(jnp.float32)).astype(jnp.bfloat16)
    for i in range(len(spans)):
        to_side(i).start()
    core_out[1] = slot_back(buddy).astype(jnp.bfloat16)
    to_core(1).start()
    mine[...] = slot_back(t)

    gate_parts[t] = jnp.broadcast_to(jnp.sum(place[...] * gate_part, axis=0, keepdims=True), (8, capacity))

    def gate_copy(i, slot):
        return pltpu.make_async_remote_copy(
            src_ref=gate_parts.at[t], dst_ref=gate_parts.at[slot], send_sem=gate_send.at[i], recv_sem=gate_recv.at[i],
            device_id=(me, mates[i]), device_id_type=MESH,
        )

    for i in range(3):
        gate_copy(i, t).start()

    def store(i):
        held, out = (
            (rows, rows_out), (dpre, dpre_out), (hidden, hidden_out), (gated, gated_out),
            (gate_held, gate_out), (token_held, token_out),
        )[i]
        return pltpu.make_async_copy(held, out, store_sem.at[i])

    gated[...] = (gate_flat * grads[...].astype(jnp.float32)).astype(jnp.bfloat16)
    for i in range(4):
        store(i).start()
    to_core(1).wait_recv()
    mine[...] += core_in[1].astype(jnp.float32)

    def total(i):
        to_side(i).wait_recv()
        return (mine[spans[i], :] + side_in[spans[i], :].astype(jnp.float32)).astype(jnp.bfloat16)

    def give_back(d, slot):
        return pltpu.make_async_remote_copy(
            src_ref=back_out.at[d], dst_ref=back_in.at[slot], send_sem=back_send.at[d], recv_sem=back_recv.at[slot],
            device_id=(d, t), device_id_type=MESH,
        )

    tail = total(0)
    packed = sum(
        contract(unpack[c * rest_rows : (c + 1) * rest_rows], tail[:, c * third : (c + 1) * third], 0, 0)
        for c in range(3)
    ).astype(jnp.bfloat16)
    back_out[:, :, pl.ds(quarter, third)] = packed.reshape(experts, 16, third)
    for i, g in enumerate(order):
        back_out[pl.ds(2 * g, 2), :, pl.ds(0, quarter)] = total(i + 1).reshape(2, 16, quarter)
        if i < 3:
            give_back(2 * g, me).start()
            give_back(2 * g + 1, me).start()
        else:
            give_back(partner, me).start()
            back_in[me] = back_out[me]
    for d in peers:
        give_back(d, d).wait_recv()
    sums = contract(picks[...], back_in[:, :, pl.ds(0, quarter)].reshape(lead_rows, quarter), 0, 0)
    returned = back_in[:, :, pl.ds(quarter, third)].reshape(lead_rows, third)
    block_id = lax.broadcasted_iota(jnp.int32, factors.shape, 1)
    pieces = []
    for c in range(3):
        piece = sums[:, c * third : (c + 1) * third] + contract(extra_picks[c], returned, 0, 0)
        factor = jnp.sum(jnp.where(block_id == 3 * t + c, factors, 0.0), axis=1, keepdims=True)
        pieces.append((piece * factor).astype(jnp.bfloat16))
    last_out[...] = jnp.concatenate(pieces, axis=1).reshape(tensors, tok_count // tensors, quarter)
    last_in[t] = last_out[t]

    def finish(i, slot):
        return pltpu.make_async_remote_copy(
            src_ref=last_out.at[mates[i]], dst_ref=last_in.at[slot], send_sem=last_send.at[i], recv_sem=last_recv.at[i],
            device_id=(me, mates[i]), device_id_type=MESH,
        )

    for i in range(3):
        finish(i, t).start()
    for i in range(3):
        gate_copy(i, mates[i]).wait_recv()
    gate_held[...] = (gate_parts[0] + gate_parts[1] + gate_parts[2] + gate_parts[3])[0:1]
    store(4).start()
    for i in range(3):
        finish(i, mates[i]).wait_recv()
    for q in range(tensors):
        token_held[:, pl.ds(q * quarter, quarter)] = last_in[q]
    store(5).start()

    for a in range(2):
        for d in peers:
            send(a, d).wait_send()
        for kind in range(3):
            for g in range(groups):
                passing(a, kind, g).wait_send()
    for i in range(2):
        to_core(i).wait_send()
    for i in range(len(spans)):
        to_side(i).wait_send()
    for d in peers:
        give_back(d, me).wait_send()
    for i in range(3):
        gate_copy(i, t).wait_send()
        finish(i, t).wait_send()
    for i in range(6):
        store(i).wait()


def exchange(experts, tensors, tokens, exponents, out_grad, slots, gates, w_in, w_out):
    tok_count, width = tokens.shape
    hid = w_in.shape[1]
    quarter = width // tensors
    wide = quarter + quarter // 3
    count = experts * 20
    bf16, f32 = jnp.bfloat16, jnp.float32
    hbm = pl.BlockSpec(memory_space=pltpu.HBM)
    dma = pltpu.SemaphoreType.DMA
    return pl.pallas_call(
        functools.partial(exchange_kernel, experts, tensors),
        out_shape=(
            jax.ShapeDtypeStruct((tok_count // tensors, width), bf16),
            jax.ShapeDtypeStruct(gates.shape, f32),
            jax.ShapeDtypeStruct((count, width), bf16),
            jax.ShapeDtypeStruct((count, width), bf16),
            jax.ShapeDtypeStruct((count, hid), bf16),
            jax.ShapeDtypeStruct((count, hid), bf16),
        ),
        in_specs=[hbm] * 7,
        out_specs=(hbm,) * 6,
        scratch_shapes=[
            pltpu.VMEM((tok_count // tensors, width), bf16),
            pltpu.VMEM(gates.shape, f32),
            pltpu.VMEM((count, width), bf16),
            pltpu.VMEM((count, width), bf16),
            pltpu.VMEM((count, hid), bf16),
            pltpu.VMEM((count, hid), bf16),
            pltpu.VMEM(tokens.shape, bf16),
            pltpu.VMEM(exponents.shape, jnp.int32),
            pltpu.VMEM(out_grad.shape, bf16),
            pltpu.VMEM(slots.shape, jnp.int32),
            pltpu.VMEM(gates.shape, f32),
            pltpu.VMEM(w_in.shape, bf16),
            pltpu.VMEM(w_out.shape, bf16),
            pltpu.VMEM((tok_count, width), bf16),
            pltpu.VMEM((experts * 16, tok_count), bf16),
            pltpu.VMEM((3, experts * 16, tok_count), bf16),
            pltpu.VMEM((count, slots.shape[1]), f32),
            pltpu.VMEM((2, experts, 16, wide), bf16),
            pltpu.VMEM((2, tensors, experts, 16, wide), bf16),
            pltpu.VMEM((count, width), bf16),
            pltpu.VMEM((count, hid), f32),
            pltpu.VMEM((2, count, quarter), bf16),
            pltpu.VMEM((2, count, quarter), bf16),
            pltpu.VMEM((count, quarter), bf16),
            pltpu.VMEM((count, quarter), bf16),
            pltpu.VMEM((count, quarter), f32),
            pltpu.VMEM((experts, 16, wide), bf16),
            pltpu.VMEM((experts, 16, wide), bf16),
            pltpu.VMEM((tensors, tok_count // tensors, quarter), bf16),
            pltpu.VMEM((tensors, tok_count // tensors, quarter), bf16),
            pltpu.VMEM((tensors, 8, slots.shape[1]), f32),
            dma((7,)),
            dma((2, experts)),
            dma((2, experts)),
            dma((2, 3, experts // 2)),
            dma((2, 3, experts // 2)),
            dma((2,)),
            dma((2,)),
            dma((5,)),
            dma((5,)),
            dma((experts,)),
            dma((experts,)),
            dma((3,)),
            dma((3,)),
            dma((3,)),
            dma((3,)),
            dma((6,)),
        ],
        compiler_params=pltpu.CompilerParams(
            collective_id=0, has_side_effects=True, vmem_limit_bytes=60 * 2**20
        ),
    )(tokens, exponents, out_grad, slots, gates, w_in, w_out)


def weights_kernel(
    token_hbm, gate_hbm, rows_hbm, gated_hbm, hidden_hbm, dpre_hbm,
    token_out, gate_out, in_out, out_out,
    rows, gated, hidden, dpre, token_held, gate_held, in_held, out_held, load_sem, sem,
):
    sources = (hidden_hbm, gated_hbm, rows_hbm, dpre_hbm, token_hbm, gate_hbm)
    helds = (hidden, gated, rows, dpre, token_held, gate_held)
    loads = [
        pltpu.make_async_copy(source, held, load_sem.at[i]) for i, (source, held) in enumerate(zip(sources, helds))
    ]
    for load in loads:
        load.start()
    chunks = 4
    copies = []
    for n, (left, right, held, out) in enumerate(((hidden, gated, out_held, out_out), (rows, dpre, in_held, in_out))):
        loads[2 * n].wait()
        loads[2 * n + 1].wait()
        for i in range(chunks):
            size = out.shape[0] // chunks
            span = pl.ds(i * size, size)
            held[span, :] = contract(left[:, span], right[...], 0, 0).astype(jnp.bfloat16)
            copies.append(pltpu.make_async_copy(held.at[span], out.at[span], sem.at[len(copies)]))
            copies[-1].start()
        if n == 0:
            for i, (held, out) in enumerate(((token_held, token_out), (gate_held, gate_out))):
                loads[4 + i].wait()
                copies.append(pltpu.make_async_copy(held, out, sem.at[len(copies)]))
                copies[-1].start()
    for copy in copies:
        copy.wait()


def weight_grads(token_grad, gate_grad, rows, gated, hidden, dpre):
    width, hid = rows.shape[1], hidden.shape[1]
    bf16 = jnp.bfloat16
    like = lambda array: jax.ShapeDtypeStruct(array.shape, array.dtype)
    hbm = pl.BlockSpec(memory_space=pltpu.HBM)
    return pl.pallas_call(
        weights_kernel,
        out_shape=(
            like(token_grad), like(gate_grad),
            jax.ShapeDtypeStruct((width, hid), bf16), jax.ShapeDtypeStruct((hid, width), bf16),
        ),
        in_specs=[hbm] * 6,
        out_specs=(hbm,) * 4,
        scratch_shapes=[
            pltpu.VMEM(array.shape, array.dtype) for array in (rows, gated, hidden, dpre, token_grad, gate_grad)
        ]
        + [
            pltpu.VMEM((width, hid), bf16),
            pltpu.VMEM((hid, width), bf16),
            pltpu.SemaphoreType.DMA((6,)),
            pltpu.SemaphoreType.DMA((10,)),
        ],
        compiler_params=pltpu.CompilerParams(vmem_limit_bytes=60 * 2**20),
    )(token_grad, gate_grad, rows, gated, hidden, dpre)


def local_fused(tokens, exponents, out_grad, slots, gates, w_in, w_out):
    results = exchange(
        lax.axis_size("expert"), lax.axis_size("tensor"),
        tokens, exponents.T, out_grad, slots, gates, w_in[0], w_out[0],
    )
    token_grad, gate_grad, in_weight_grad, out_weight_grad = weight_grads(*results)
    return (token_grad, in_weight_grad[None], out_weight_grad[None], gate_grad)


def fits_exchange(mesh):
    return mesh.shape["expert"] == 8 and mesh.shape["tensor"] == 4


def solution(mesh):
    placed = (
        P("expert", None),
        P("expert", None),
        P("expert", None),
        P(),
        P("expert", None),
        P("expert", None, "tensor"),
        P("expert", "tensor", None),
    )
    return jax.shard_map(
        local_fused if fits_exchange(mesh) else local,
        mesh=mesh,
        in_specs=placed,
        out_specs=(
            P(("expert", "tensor"), None),
            P("expert", None, "tensor"),
            P("expert", "tensor", None),
            P("expert", None),
        ),
        check_vma=False,
    )
```

profile of v0, /device:TPU:0, one launch (start us, length us, event | category | flops | bytes accessed | tf_op | source)
XLA Modules:
  0.0 40.7 jit_solution(1373235508501949011)
XLA Ops:
  0.6 35.7 %shard_map.102 = (bf16[16,1536]{1,0:T(8,128)(2,1)}, f32[1,128]{1,0:T(1,128)}, bf16[160,1536]{1,0:T(8,128)(2,1)}, bf16[160,1536]{1,0:T(8,128)(2,1)}, bf16[160,102...) custom-call(bf16[64,1536]{1,0:T(8,128)(2,1)} %tokens_hbm.1, s32[12,64]{1,0:T(8,128)} %bitcast.7, bf16[64,1536]{1,0:T(8,128)(2,1)} %out_grad_hbm.1, ...), custom_call_target="tpu_custom_call" | custom-call | tf_op jit(solution)/shard_map/pallas_call | solution.py:459
  36.3 4.4 %shard_map.103 = (bf16[16,1536]{1,0:T(8,128)(2,1)}, f32[1,128]{1,0:T(1,128)}, bf16[1536,1024]{1,0:T(8,128)(2,1)}, bf16[1024,1536]{1,0:T(8,128)(2,1)}) custom-call(bf16[16,1536]{1,0:T(8,128)(2,1)} %get-tuple-element.14.token_hbm, f32[1,128]{1,0:T(1,128)} %get-tuple-element.15.gate_hbm, bf16[160,1536]{1,0:T(8,128)(2,1)} %get-tuple-element.16.rows_hbm, ...), custom_call_target="tpu_custom_call" | custom-call | tf_op jit(solution)/shard_map/pallas_call | solution.py:563
where the time goes:
time: 40.9 us; the launch traced here: 40.7 us
  Pallas kernels  40.1 us (98%)
  between operations  0.64 us (2%)
    pallas_call x1, Pallas kernels, exchange(): pl.pallas_call(functools.partial(exchange_kernel, experts, tensors), out_...  35.7 us
    pallas_call x1, Pallas kernels, weight_grads(): pl.pallas_call(weights_kernel, out_shape=(like(token_grad), like(gate_gra...  4.35 us

commit v1 on v0

--- a/solution.py
+++ b/solution.py
@@ -108,10 +108,10 @@
 def exchange_kernel(
     experts, tensors,
     tokens_hbm, exponents_hbm, out_grad_hbm, slots_hbm, gates_hbm, w_in_hbm, w_out_hbm,
-    token_out, gate_out, rows_out, gated_out, hidden_out, dpre_out,
+    token_out, gate_out, rows_out, dpre_out, weight_out,
     token_held, gate_held, rows, gated, hidden, dpre,
     tokens, exponents, out_grad, slots, gates,
-    w_in, w_out, scaled, picks, extra_picks, place, outgoing, parts, grads, preact,
+    w_in, w_out, scaled, picks, extra_picks, place, outgoing, parts, grads, slope, upstream, weight_held,
     core_out, core_in, side_out, side_in, mine, back_out, back_in, last_out, last_in, gate_parts,
     load_sem, send_sem, recv_sem, pass_send, pass_recv, ret_send, ret_recv, side_send, side_recv,
     back_send, back_recv, last_send, last_recv, gate_send, gate_recv, store_sem,
@@ -262,61 +262,73 @@
         return pl.ds(pl.multiple_of(i * hidden_block, hidden_block), hidden_block)
 
     near_first = [order[3], order[2], order[0], order[1]]
-    for a in range(2):
-        for i, g in enumerate(near_first):
-            if i == 0:
-                arrival(a, partner).wait_recv()
-            else:
-                arrival(a, 2 * g).wait_recv()
-                arrival(a, 2 * g + 1).wait_recv()
-            passing(a, 1, g).start()
-            passing(a, 0, g).start()
+
+    def take(a, g):
+        if g is order[3]:
+            arrival(a, partner).wait_recv()
+        else:
+            arrival(a, 2 * g).wait_recv()
+            arrival(a, 2 * g + 1).wait_recv()
+        passing(a, 1, g).start()
+        passing(a, 0, g).start()
 
     def relay(a, g):
         passed(a, 1, g).wait_recv()
         passing(a, 2, g).start()
 
-    def arrange(a, target):
-        for g in near_first:
-            passed(a, 0, g).wait_recv()
-        for g in near_first:
-            passed(a, 2, g).wait_recv()
-        for q in range(tensors):
-            target[pl.ds(0, lead_rows), pl.ds(q * quarter, quarter)] = parts[a, q, :, :, pl.ds(0, quarter)].reshape(
-                lead_rows, quarter
-            )
-            rest = jnp.dot(
-                unpack, parts[a, q, :, :, pl.ds(quarter, third)].reshape(lead_rows, third),
-                preferred_element_type=jnp.float32,
-            ).astype(jnp.bfloat16)
-            for c in range(3):
-                target[pl.ds(lead_rows, rest_rows), pl.ds(q * quarter + c * third, third)] = rest[
-                    c * rest_rows : (c + 1) * rest_rows
-                ]
-
+    def arrange(a, q, target):
+        cols = pl.ds(pl.multiple_of(q * quarter, 128), quarter)
+        target[pl.ds(0, lead_rows), cols] = parts[a, q, :, :, pl.ds(0, quarter)].reshape(lead_rows, quarter)
+        rest = jnp.dot(
+            unpack, parts[a, q, :, :, pl.ds(quarter, third)].reshape(lead_rows, third),
+            preferred_element_type=jnp.float32,
+        ).astype(jnp.bfloat16)
+        for c in range(3):
+            some = pl.ds(pl.multiple_of(q * quarter + c * third, 128), third)
+            target[pl.ds(lead_rows, rest_rows), some] = rest[c * rest_rows : (c + 1) * rest_rows]
+        return cols
+
+    for g in near_first:
+        take(0, g)
+    for g in near_first[:2]:
+        take(1, g)
     for g in near_first:
         relay(0, g)
-    arrange(0, rows)
+    for g in near_first[2:]:
+        take(1, g)
+    for kind in (0, 2):
+        for g in near_first:
+            passed(0, kind, g).wait_recv()
+    for q in range(tensors):
+        arrange(0, q, rows)
     loads[5].wait()
     for i, g in enumerate(near_first):
         cols = pl.ds(i * hidden_block, hidden_block)
-        preact[:, cols] = jnp.dot(rows[...], w_in[:, cols], preferred_element_type=jnp.float32)
+        v = jnp.dot(rows[...], w_in[:, cols], preferred_element_type=jnp.float32)
         relay(1, g)
-    arrange(1, grads)
-    loads[6].wait()
-
-    def backward(i, total):
-        cols = block_of(i)
-        v = preact[:, cols]
-        upstream = contract(grads[...], w_out[cols, :], 1, 1)
         square = v * v
         tanh = jnp.tanh(ROOT * (v + CUBIC * v * square))
         half = 0.5 * (1.0 + tanh)
-        act = (v * half).astype(jnp.bfloat16)
-        slope = half + 0.5 * v * (1.0 - tanh * tanh) * (ROOT * (1.0 + 3.0 * CUBIC * square))
-        hidden[:, cols] = act
-        dpre[:, cols] = (gate_flat * upstream * slope).astype(jnp.bfloat16)
-        return total + jnp.sum(act.astype(jnp.float32) * upstream, axis=1, keepdims=True)
+        hidden[:, cols] = (v * half).astype(jnp.bfloat16)
+        slope[:, cols] = half + 0.5 * v * (1.0 - tanh * tanh) * (ROOT * (1.0 + 3.0 * CUBIC * square))
+
+    loads[6].wait()
+    for i, (q, kind) in enumerate(((t, None), (buddy, 0), (across, None))):
+        if kind is not None:
+            for g in near_first:
+                passed(1, kind, g).wait_recv()
+        part = arrange(1, q, grads)
+        term = contract(grads[:, part], w_out[:, part], 1, 1)
+        upstream[...] = term if i == 0 else upstream[...] + term
+    for g in near_first:
+        passed(1, 2, g).wait_recv()
+    last_part = arrange(1, diagonal, grads)
+
+    def backward(i, total):
+        cols = block_of(i)
+        up = upstream[:, cols] + contract(grads[:, last_part], w_out[cols, last_part], 1, 1)
+        dpre[:, cols] = (gate_flat * up * slope[:, cols]).astype(jnp.bfloat16)
+        return total + jnp.sum(hidden[:, cols].astype(jnp.float32) * up, axis=1, keepdims=True)
 
     gate_part = lax.fori_loop(0, groups, backward, jnp.zeros((place.shape[0], 1), jnp.float32))
 
@@ -362,13 +374,12 @@
 
     def store(i):
         held, out = (
-            (rows, rows_out), (dpre, dpre_out), (hidden, hidden_out), (gated, gated_out),
-            (gate_held, gate_out), (token_held, token_out),
+            (rows, rows_out), (dpre, dpre_out), (gate_held, gate_out), (token_held, token_out),
         )[i]
         return pltpu.make_async_copy(held, out, store_sem.at[i])
 
     gated[...] = (gate_flat * grads[...].astype(jnp.float32)).astype(jnp.bfloat16)
-    for i in range(4):
+    for i in range(2):
         store(i).start()
     to_core(1).wait_recv()
     mine[...] += core_in[1].astype(jnp.float32)
@@ -397,6 +408,15 @@
         else:
             give_back(partner, me).start()
             back_in[me] = back_out[me]
+
+    def store_weight(i):
+        span = pl.ds(i * hidden_block, hidden_block)
+        return pltpu.make_async_copy(weight_held.at[span], weight_out.at[span], store_sem.at[4 + i])
+
+    for i in range(groups):
+        span = pl.ds(i * hidden_block, hidden_block)
+        weight_held[span, :] = contract(hidden[:, span], gated[...], 0, 0).astype(jnp.bfloat16)
+        store_weight(i).start()
     for d in peers:
         give_back(d, d).wait_recv()
     sums = contract(picks[...], back_in[:, :, pl.ds(0, quarter)].reshape(lead_rows, quarter), 0, 0)
@@ -421,12 +441,12 @@
     for i in range(3):
         gate_copy(i, mates[i]).wait_recv()
     gate_held[...] = (gate_parts[0] + gate_parts[1] + gate_parts[2] + gate_parts[3])[0:1]
-    store(4).start()
+    store(2).start()
     for i in range(3):
         finish(i, mates[i]).wait_recv()
     for q in range(tensors):
         token_held[:, pl.ds(q * quarter, quarter)] = last_in[q]
-    store(5).start()
+    store(3).start()
 
     for a in range(2):
         for d in peers:
@@ -443,8 +463,10 @@
     for i in range(3):
         gate_copy(i, t).wait_send()
         finish(i, t).wait_send()
-    for i in range(6):
+    for i in range(4):
         store(i).wait()
+    for i in range(groups):
+        store_weight(i).wait()
 
 
 def exchange(experts, tensors, tokens, exponents, out_grad, slots, gates, w_in, w_out):
@@ -462,12 +484,11 @@
             jax.ShapeDtypeStruct((tok_count // tensors, width), bf16),
             jax.ShapeDtypeStruct(gates.shape, f32),
             jax.ShapeDtypeStruct((count, width), bf16),
-            jax.ShapeDtypeStruct((count, width), bf16),
             jax.ShapeDtypeStruct((count, hid), bf16),
-            jax.ShapeDtypeStruct((count, hid), bf16),
+            jax.ShapeDtypeStruct((hid, width), bf16),
         ),
         in_specs=[hbm] * 7,
-        out_specs=(hbm,) * 6,
+        out_specs=(hbm,) * 5,
         scratch_shapes=[
             pltpu.VMEM((tok_count // tensors, width), bf16),
             pltpu.VMEM(gates.shape, f32),
@@ -490,6 +511,8 @@
             pltpu.VMEM((2, tensors, experts, 16, wide), bf16),
             pltpu.VMEM((count, width), bf16),
             pltpu.VMEM((count, hid), f32),
+            pltpu.VMEM((count, hid), f32),
+            pltpu.VMEM((hid, width), bf16),
             pltpu.VMEM((2, count, quarter), bf16),
             pltpu.VMEM((2, count, quarter), bf16),
             pltpu.VMEM((count, quarter), bf16),
@@ -515,7 +538,7 @@
             dma((3,)),
             dma((3,)),
             dma((3,)),
-            dma((6,)),
+            dma((8,)),
         ],
         compiler_params=pltpu.CompilerParams(
             collective_id=0, has_side_effects=True, vmem_limit_bytes=60 * 2**20
@@ -524,12 +547,12 @@
 
 
 def weights_kernel(
-    token_hbm, gate_hbm, rows_hbm, gated_hbm, hidden_hbm, dpre_hbm,
-    token_out, gate_out, in_out, out_out,
-    rows, gated, hidden, dpre, token_held, gate_held, in_held, out_held, load_sem, sem,
+    token_hbm, gate_hbm, rows_hbm, dpre_hbm, weight_hbm,
+    token_out, gate_out, in_out, weight_out,
+    rows, dpre, token_held, gate_held, in_held, load_sem, sem,
 ):
-    sources = (hidden_hbm, gated_hbm, rows_hbm, dpre_hbm, token_hbm, gate_hbm)
-    helds = (hidden, gated, rows, dpre, token_held, gate_held)
+    sources = (rows_hbm, dpre_hbm, token_hbm, gate_hbm)
+    helds = (rows, dpre, token_held, gate_held)
     loads = [
         pltpu.make_async_copy(source, held, load_sem.at[i]) for i, (source, held) in enumerate(zip(sources, helds))
     ]
@@ -537,48 +560,49 @@
         load.start()
     chunks = 4
     copies = []
-    for n, (left, right, held, out) in enumerate(((hidden, gated, out_held, out_out), (rows, dpre, in_held, in_out))):
-        loads[2 * n].wait()
-        loads[2 * n + 1].wait()
-        for i in range(chunks):
-            size = out.shape[0] // chunks
-            span = pl.ds(i * size, size)
-            held[span, :] = contract(left[:, span], right[...], 0, 0).astype(jnp.bfloat16)
-            copies.append(pltpu.make_async_copy(held.at[span], out.at[span], sem.at[len(copies)]))
-            copies[-1].start()
-        if n == 0:
-            for i, (held, out) in enumerate(((token_held, token_out), (gate_held, gate_out))):
-                loads[4 + i].wait()
-                copies.append(pltpu.make_async_copy(held, out, sem.at[len(copies)]))
-                copies[-1].start()
-    for copy in copies:
-        copy.wait()
-
-
-def weight_grads(token_grad, gate_grad, rows, gated, hidden, dpre):
-    width, hid = rows.shape[1], hidden.shape[1]
-    bf16 = jnp.bfloat16
+
+    def copy(source, target):
+        copies.append(pltpu.make_async_copy(source, target, sem.at[len(copies)]))
+        copies[-1].start()
+
+    for i in range(chunks):
+        size = weight_out.shape[0] // chunks
+        span = pl.ds(i * size, size)
+        copy(weight_hbm.at[span], weight_out.at[span])
+    loads[0].wait()
+    loads[1].wait()
+    for i in range(chunks):
+        size = in_out.shape[0] // chunks
+        span = pl.ds(i * size, size)
+        in_held[span, :] = contract(rows[:, span], dpre[...], 0, 0).astype(jnp.bfloat16)
+        copy(in_held.at[span], in_out.at[span])
+    for i, target in ((2, token_out), (3, gate_out)):
+        loads[i].wait()
+        copy(helds[i], target)
+    for each in copies:
+        each.wait()
+
+
+def weight_grads(token_grad, gate_grad, rows, dpre, out_weight_grad):
+    width, hid = rows.shape[1], dpre.shape[1]
     like = lambda array: jax.ShapeDtypeStruct(array.shape, array.dtype)
     hbm = pl.BlockSpec(memory_space=pltpu.HBM)
     return pl.pallas_call(
         weights_kernel,
         out_shape=(
             like(token_grad), like(gate_grad),
-            jax.ShapeDtypeStruct((width, hid), bf16), jax.ShapeDtypeStruct((hid, width), bf16),
+            jax.ShapeDtypeStruct((width, hid), jnp.bfloat16), like(out_weight_grad),
         ),
-        in_specs=[hbm] * 6,
+        in_specs=[hbm] * 5,
         out_specs=(hbm,) * 4,
-        scratch_shapes=[
-            pltpu.VMEM(array.shape, array.dtype) for array in (rows, gated, hidden, dpre, token_grad, gate_grad)
-        ]
+        scratch_shapes=[pltpu.VMEM(array.shape, array.dtype) for array in (rows, dpre, token_grad, gate_grad)]
         + [
-            pltpu.VMEM((width, hid), bf16),
-            pltpu.VMEM((hid, width), bf16),
-            pltpu.SemaphoreType.DMA((6,)),
+            pltpu.VMEM((width, hid), jnp.bfloat16),
+            pltpu.SemaphoreType.DMA((4,)),
             pltpu.SemaphoreType.DMA((10,)),
         ],
         compiler_params=pltpu.CompilerParams(vmem_limit_bytes=60 * 2**20),
-    )(token_grad, gate_grad, rows, gated, hidden, dpre)
+    )(token_grad, gate_grad, rows, dpre, out_weight_grad)
 
 
 def local_fused(tokens, exponents, out_grad, slots, gates, w_in, w_out):

time: 40.9 us -> 134 us (3.28)
  Pallas kernels: 40.1 us -> 133 us
    pallas_call x1, Pallas kernels: 4.35 us -> 96.5 us  [weight_grads(): pl.pallas_call(weights_kernel, out_shape=(like(token_grad), like(gate_gra...]
where the time goes in v1:
time: 134 us
  Pallas kernels  133 us (99%)
    pallas_call x1, Pallas kernels, weight_grads(): pl.pallas_call(weights_kernel, out_shape=(like(token_grad), like(gate_gra...  96.5 us
    pallas_call x1, Pallas kernels, exchange(): pl.pallas_call(functools.partial(exchange_kernel, experts, tensors), out_...  36.7 us

profile of v1, /device:TPU:0, one launch (start us, length us, event | category | flops | bytes accessed | tf_op | source)
XLA Modules:
  0.0 133.8 jit_solution(13781416455008970436)
XLA Ops:
  0.6 36.7 %shard_map.102 = (bf16[16,1536]{1,0:T(8,128)(2,1)}, f32[1,128]{1,0:T(1,128)}, bf16[160,1536]{1,0:T(8,128)(2,1)}, bf16[160,1024]{1,0:T(8,128)(2,1)}, bf16[1024,1536]{1,0:T(8,128)(2,1)}) custom-call(bf16[64,1536]{1,0:T(8,128)(2,1)} %tokens_hbm.1, s32[12,64]{1,0:T(8,128)} %bitcast.7, bf16[64,1536]{1,0:T(8,128)(2,1)} %out_grad_hbm.1, s32[8,128]{1,0:T(8,128)} %slots_hbm.1, ...), custom_call_target="tpu_custom_call" | custom-call | tf_op jit(solution)/shard_map/pallas_call | solution.py:481
  37.3 96.5 %shard_map.103 = (bf16[16,1536]{1,0:T(8,128)(2,1)}, f32[1,128]{1,0:T(1,128)}, bf16[1536,1024]{1,0:T(8,128)(2,1)}, bf16[1024,1536]{1,0:T(8,128)(2,1)}) custom-call(bf16[16,1536]{1,0:T(8,128)(2,1)} %get-tuple-element.13.token_hbm, f32[1,128]{1,0:T(1,128)} %get-tuple-element.14.gate_hbm, bf16[160,1536]{1,0:T(8,128)(2,1)} %get-tuple-element.15.rows_hbm, ...), custom_call_target="tpu_custom_call" | custom-call | tf_op jit(solution)/shard_map/pallas_call | solution.py:590

commit v2 on v1

--- a/solution.py
+++ b/solution.py
@@ -108,10 +108,10 @@
 def exchange_kernel(
     experts, tensors,
     tokens_hbm, exponents_hbm, out_grad_hbm, slots_hbm, gates_hbm, w_in_hbm, w_out_hbm,
-    token_out, gate_out, rows_out, dpre_out, weight_out,
+    token_out, gate_out, rows_out, gated_out, hidden_out, dpre_out,
     token_held, gate_held, rows, gated, hidden, dpre,
     tokens, exponents, out_grad, slots, gates,
-    w_in, w_out, scaled, picks, extra_picks, place, outgoing, parts, grads, slope, upstream, weight_held,
+    w_in, w_out, picks, extra_picks, place, outgoing, parts, grads, slope, upstream,
     core_out, core_in, side_out, side_in, mine, back_out, back_in, last_out, last_in, gate_parts,
     load_sem, send_sem, recv_sem, pass_send, pass_recv, ret_send, ret_recv, side_send, side_recv,
     back_send, back_recv, last_send, last_recv, gate_send, gate_recv, store_sem,
@@ -137,7 +137,7 @@
             )
         )
     ]
-    for load in loads:
+    for load in loads[:5]:
         load.start()
 
     barrier = pltpu.get_barrier_semaphore()
@@ -182,22 +182,20 @@
             extra_picks[c, span, :] = jnp.where(part_id == c, rest_hit, 0.0).astype(jnp.bfloat16)
 
     blocks = exponents.shape[0]
-    eye = (
-        lax.broadcasted_iota(jnp.int32, (blocks, blocks), 0) == lax.broadcasted_iota(jnp.int32, (blocks, blocks), 1)
+    chosen = (
+        lax.broadcasted_iota(jnp.int32, (blocks, 4), 0) == 3 * t + lax.broadcasted_iota(jnp.int32, (blocks, 4), 1)
     ).astype(jnp.bfloat16)
     loads[1].wait()
-    factors = contract(jnp.exp2(exponents[...].astype(jnp.float32)).astype(jnp.bfloat16), eye, 0, 0)
-    loads[2].wait()
-    for b in range(width // 128):
-        cols = pl.ds(b * 128, 128)
-        scaled[:, cols] = (tokens[:, cols].astype(jnp.float32) * factors[:, b : b + 1]).astype(jnp.bfloat16)
-
-    loads[3].wait()
+    factors = contract(jnp.exp2(exponents[...].astype(jnp.float32)).astype(jnp.bfloat16), chosen, 0, 0)
     my_cols = pl.ds(pl.multiple_of(t * quarter, 128), quarter)
-    for a, source in enumerate((scaled, out_grad)):
-        filled = message(picks[...], extra_picks[...], source[:, my_cols])
-        outgoing[a] = filled.reshape(experts, 16, 4 * third)
-    for a in range(2):
+
+    def scale(values):
+        return jnp.concatenate(
+            [values[:, c * third : (c + 1) * third] * factors[:, c : c + 1] for c in range(3)], axis=1
+        ).astype(jnp.bfloat16)
+
+    def fill(a, mine_here):
+        outgoing[a] = message(picks[...], extra_picks[...], mine_here).reshape(experts, 16, 4 * third)
         parts[a, t, me] = outgoing[a, me]
 
     def send(a, d):
@@ -234,10 +232,17 @@
             device_id=(me, mate), device_id_type=MESH,
         )
 
+    loads[2].wait()
+    fill(0, scale(tokens[:, my_cols].astype(jnp.float32)))
     pl.semaphore_wait(barrier, len(peers) + len(mates))
-    for a in range(2):
-        for d in peers:
-            send(a, d).start()
+    for d in peers:
+        send(0, d).start()
+    loads[3].wait()
+    fill(1, out_grad[:, my_cols])
+    for d in peers:
+        send(1, d).start()
+    for load in loads[5:]:
+        load.start()
 
     my_slots = slots[pl.ds(me, 1), :] // tok_count
     owner_id = lax.broadcasted_iota(jnp.int32, (experts, capacity), 0)
@@ -262,6 +267,13 @@
         return pl.ds(pl.multiple_of(i * hidden_block, hidden_block), hidden_block)
 
     near_first = [order[3], order[2], order[0], order[1]]
+
+    def store(i):
+        held, out = (
+            (gate_held, gate_out), (token_held, token_out),
+            (rows, rows_out), (hidden, hidden_out), (gated, gated_out), (dpre, dpre_out),
+        )[i]
+        return pltpu.make_async_copy(held, out, store_sem.at[i])
 
     def take(a, g):
         if g is order[3]:
@@ -312,6 +324,9 @@
         hidden[:, cols] = (v * half).astype(jnp.bfloat16)
         slope[:, cols] = half + 0.5 * v * (1.0 - tanh * tanh) * (ROOT * (1.0 + 3.0 * CUBIC * square))
 
+    store(2).start()
+    store(3).start()
+
     loads[6].wait()
     for i, (q, kind) in enumerate(((t, None), (buddy, 0), (across, None))):
         if kind is not None:
@@ -372,15 +387,7 @@
     for i in range(3):
         gate_copy(i, t).start()
 
-    def store(i):
-        held, out = (
-            (rows, rows_out), (dpre, dpre_out), (gate_held, gate_out), (token_held, token_out),
-        )[i]
-        return pltpu.make_async_copy(held, out, store_sem.at[i])
-
     gated[...] = (gate_flat * grads[...].astype(jnp.float32)).astype(jnp.bfloat16)
-    for i in range(2):
-        store(i).start()
     to_core(1).wait_recv()
     mine[...] += core_in[1].astype(jnp.float32)
 
@@ -408,46 +415,8 @@
         else:
             give_back(partner, me).start()
             back_in[me] = back_out[me]
-
-    def store_weight(i):
-        span = pl.ds(i * hidden_block, hidden_block)
-        return pltpu.make_async_copy(weight_held.at[span], weight_out.at[span], store_sem.at[4 + i])
-
-    for i in range(groups):
-        span = pl.ds(i * hidden_block, hidden_block)
-        weight_held[span, :] = contract(hidden[:, span], gated[...], 0, 0).astype(jnp.bfloat16)
-        store_weight(i).start()
-    for d in peers:
-        give_back(d, d).wait_recv()
-    sums = contract(picks[...], back_in[:, :, pl.ds(0, quarter)].reshape(lead_rows, quarter), 0, 0)
-    returned = back_in[:, :, pl.ds(quarter, third)].reshape(lead_rows, third)
-    block_id = lax.broadcasted_iota(jnp.int32, factors.shape, 1)
-    pieces = []
-    for c in range(3):
-        piece = sums[:, c * third : (c + 1) * third] + contract(extra_picks[c], returned, 0, 0)
-        factor = jnp.sum(jnp.where(block_id == 3 * t + c, factors, 0.0), axis=1, keepdims=True)
-        pieces.append((piece * factor).astype(jnp.bfloat16))
-    last_out[...] = jnp.concatenate(pieces, axis=1).reshape(tensors, tok_count // tensors, quarter)
-    last_in[t] = last_out[t]
-
-    def finish(i, slot):
-        return pltpu.make_async_remote_copy(
-            src_ref=last_out.at[mates[i]], dst_ref=last_in.at[slot], send_sem=last_send.at[i], recv_sem=last_recv.at[i],
-            device_id=(me, mates[i]), device_id_type=MESH,
-        )
-
-    for i in range(3):
-        finish(i, t).start()
-    for i in range(3):
-        gate_copy(i, mates[i]).wait_recv()
-    gate_held[...] = (gate_parts[0] + gate_parts[1] + gate_parts[2] + gate_parts[3])[0:1]
-    store(2).start()
-    for i in range(3):
-        finish(i, mates[i]).wait_recv()
-    for q in range(tensors):
-        token_held[:, pl.ds(q * quarter, quarter)] = last_in[q]
-    store(3).start()
-
+    store(4).start()
+    store(5).start()
     for a in range(2):
         for d in peers:
             send(a, d).wait_send()
@@ -459,14 +428,40 @@
     for i in range(len(spans)):
         to_side(i).wait_send()
     for d in peers:
+        give_back(d, d).wait_recv()
+    sums = contract(picks[...], back_in[:, :, pl.ds(0, quarter)].reshape(lead_rows, quarter), 0, 0)
+    returned = back_in[:, :, pl.ds(quarter, third)].reshape(lead_rows, third)
+    pieces = [
+        sums[:, c * third : (c + 1) * third] + contract(extra_picks[c], returned, 0, 0) for c in range(3)
+    ]
+    last_out[...] = scale(jnp.concatenate(pieces, axis=1)).reshape(tensors, tok_count // tensors, quarter)
+    last_in[t] = last_out[t]
+
+    def finish(i, slot):
+        return pltpu.make_async_remote_copy(
+            src_ref=last_out.at[mates[i]], dst_ref=last_in.at[slot], send_sem=last_send.at[i], recv_sem=last_recv.at[i],
+            device_id=(me, mates[i]), device_id_type=MESH,
+        )
+
+    for i in range(3):
+        finish(i, t).start()
+    for i in range(3):
+        gate_copy(i, mates[i]).wait_recv()
+    gate_held[...] = (gate_parts[0] + gate_parts[1] + gate_parts[2] + gate_parts[3])[0:1]
+    store(0).start()
+    for i in range(3):
+        finish(i, mates[i]).wait_recv()
+    for q in range(tensors):
+        token_held[:, pl.ds(q * quarter, quarter)] = last_in[q]
+    store(1).start()
+
+    for d in peers:
         give_back(d, me).wait_send()
     for i in range(3):
         gate_copy(i, t).wait_send()
         finish(i, t).wait_send()
-    for i in range(4):
+    for i in range(6):
         store(i).wait()
-    for i in range(groups):
-        store_weight(i).wait()
 
 
 def exchange(experts, tensors, tokens, exponents, out_grad, slots, gates, w_in, w_out):
@@ -484,11 +479,12 @@
             jax.ShapeDtypeStruct((tok_count // tensors, width), bf16),
             jax.ShapeDtypeStruct(gates.shape, f32),
             jax.ShapeDtypeStruct((count, width), bf16),
+            jax.ShapeDtypeStruct((count, width), bf16),
             jax.ShapeDtypeStruct((count, hid), bf16),
-            jax.ShapeDtypeStruct((hid, width), bf16),
+            jax.ShapeDtypeStruct((count, hid), bf16),
         ),
         in_specs=[hbm] * 7,
-        out_specs=(hbm,) * 5,
+        out_specs=(hbm,) * 6,
         scratch_shapes=[
             pltpu.VMEM((tok_count // tensors, width), bf16),
             pltpu.VMEM(gates.shape, f32),
@@ -503,7 +499,6 @@
             pltpu.VMEM(gates.shape, f32),
             pltpu.VMEM(w_in.shape, bf16),
             pltpu.VMEM(w_out.shape, bf16),
-            pltpu.VMEM((tok_count, width), bf16),
             pltpu.VMEM((experts * 16, tok_count), bf16),
             pltpu.VMEM((3, experts * 16, tok_count), bf16),
             pltpu.VMEM((count, slots.shape[1]), f32),
@@ -512,7 +507,6 @@
             pltpu.VMEM((count, width), bf16),
             pltpu.VMEM((count, hid), f32),
             pltpu.VMEM((count, hid), f32),
-            pltpu.VMEM((hid, width), bf16),
             pltpu.VMEM((2, count, quarter), bf16),
             pltpu.VMEM((2, count, quarter), bf16),
             pltpu.VMEM((count, quarter), bf16),
@@ -538,7 +532,7 @@
             dma((3,)),
             dma((3,)),
             dma((3,)),
-            dma((8,)),
+            dma((6,)),
         ],
         compiler_params=pltpu.CompilerParams(
             collective_id=0, has_side_effects=True, vmem_limit_bytes=60 * 2**20
@@ -547,12 +541,12 @@
 
 
 def weights_kernel(
-    token_hbm, gate_hbm, rows_hbm, dpre_hbm, weight_hbm,
-    token_out, gate_out, in_out, weight_out,
-    rows, dpre, token_held, gate_held, in_held, load_sem, sem,
+    token_hbm, gate_hbm, rows_hbm, gated_hbm, hidden_hbm, dpre_hbm,
+    token_out, gate_out, in_out, out_out,
+    rows, gated, hidden, dpre, token_held, gate_held, in_held, out_held, load_sem, sem,
 ):
-    sources = (rows_hbm, dpre_hbm, token_hbm, gate_hbm)
-    helds = (rows, dpre, token_held, gate_held)
+    sources = (hidden_hbm, gated_hbm, rows_hbm, dpre_hbm, token_hbm, gate_hbm)
+    helds = (hidden, gated, rows, dpre, token_held, gate_held)
     loads = [
         pltpu.make_async_copy(source, held, load_sem.at[i]) for i, (source, held) in enumerate(zip(sources, helds))
     ]
@@ -560,49 +554,48 @@
         load.start()
     chunks = 4
     copies = []
-
-    def copy(source, target):
-        copies.append(pltpu.make_async_copy(source, target, sem.at[len(copies)]))
-        copies[-1].start()
-
-    for i in range(chunks):
-        size = weight_out.shape[0] // chunks
-        span = pl.ds(i * size, size)
-        copy(weight_hbm.at[span], weight_out.at[span])
-    loads[0].wait()
-    loads[1].wait()
-    for i in range(chunks):
-        size = in_out.shape[0] // chunks
-        span = pl.ds(i * size, size)
-        in_held[span, :] = contract(rows[:, span], dpre[...], 0, 0).astype(jnp.bfloat16)
-        copy(in_held.at[span], in_out.at[span])
-    for i, target in ((2, token_out), (3, gate_out)):
-        loads[i].wait()
-        copy(helds[i], target)
-    for each in copies:
-        each.wait()
-
-
-def weight_grads(token_grad, gate_grad, rows, dpre, out_weight_grad):
-    width, hid = rows.shape[1], dpre.shape[1]
+    for n, (left, right, held, out) in enumerate(((hidden, gated, out_held, out_out), (rows, dpre, in_held, in_out))):
+        loads[2 * n].wait()
+        loads[2 * n + 1].wait()
+        for i in range(chunks):
+            size = out.shape[0] // chunks
+            span = pl.ds(i * size, size)
+            held[span, :] = contract(left[:, span], right[...], 0, 0).astype(jnp.bfloat16)
+            copies.append(pltpu.make_async_copy(held.at[span], out.at[span], sem.at[len(copies)]))
+            copies[-1].start()
+        if n == 0:
+            for i, (held, out) in enumerate(((token_held, token_out), (gate_held, gate_out))):
+                loads[4 + i].wait()
+                copies.append(pltpu.make_async_copy(held, out, sem.at[len(copies)]))
+                copies[-1].start()
+    for copy in copies:
+        copy.wait()
+
+
+def weight_grads(token_grad, gate_grad, rows, gated, hidden, dpre):
+    width, hid = rows.shape[1], hidden.shape[1]
+    bf16 = jnp.bfloat16
     like = lambda array: jax.ShapeDtypeStruct(array.shape, array.dtype)
     hbm = pl.BlockSpec(memory_space=pltpu.HBM)
     return pl.pallas_call(
         weights_kernel,
         out_shape=(
             like(token_grad), like(gate_grad),
-            jax.ShapeDtypeStruct((width, hid), jnp.bfloat16), like(out_weight_grad),
+            jax.ShapeDtypeStruct((width, hid), bf16), jax.ShapeDtypeStruct((hid, width), bf16),
         ),
-        in_specs=[hbm] * 5,
+        in_specs=[hbm] * 6,
         out_specs=(hbm,) * 4,
-        scratch_shapes=[pltpu.VMEM(array.shape, array.dtype) for array in (rows, dpre, token_grad, gate_grad)]
+        scratch_shapes=[
+            pltpu.VMEM(array.shape, array.dtype) for array in (rows, gated, hidden, dpre, token_grad, gate_grad)
+        ]
         + [
-            pltpu.VMEM((width, hid), jnp.bfloat16),
-            pltpu.SemaphoreType.DMA((4,)),
+            pltpu.VMEM((width, hid), bf16),
+            pltpu.VMEM((hid, width), bf16),
+            pltpu.SemaphoreType.DMA((6,)),
             pltpu.SemaphoreType.DMA((10,)),
         ],
         compiler_params=pltpu.CompilerParams(vmem_limit_bytes=60 * 2**20),
-    )(token_grad, gate_grad, rows, dpre, out_weight_grad)
+    )(token_grad, gate_grad, rows, gated, hidden, dpre)
 
 
 def local_fused(tokens, exponents, out_grad, slots, gates, w_in, w_out):

time: 134 us -> 41.8 us (0.31)
  Pallas kernels: 133 us -> 41 us
    pallas_call x1, Pallas kernels: 96.5 us -> 4.35 us  [weight_grads(): pl.pallas_call(weights_kernel, out_shape=(like(token_grad), like(gate_gra...]
where the time goes in v2:
time: 41.8 us; the launch traced here: 41.6 us
  Pallas kernels  41 us (98%)
  between operations  0.64 us (2%)
    pallas_call x1, Pallas kernels, exchange(): pl.pallas_call(functools.partial(exchange_kernel, experts, tensors), out_...  36.6 us
    pallas_call x1, Pallas kernels, weight_grads(): pl.pallas_call(weights_kernel, out_shape=(like(token_grad), like(gate_gra...  4.35 us

profile of v2, /device:TPU:0, one launch (start us, length us, event | category | flops | bytes accessed | tf_op | source)
XLA Modules:
  0.0 41.6 jit_solution(10315636283306790803)
XLA Ops:
  0.6 36.6 %shard_map.102 = (bf16[16,1536]{1,0:T(8,128)(2,1)}, f32[1,128]{1,0:T(1,128)}, bf16[160,1536]{1,0:T(8,128)(2,1)}, bf16[160,1536]{1,0:T(8,128)(2,1)}, bf16[160,102...) custom-call(bf16[64,1536]{1,0:T(8,128)(2,1)} %tokens_hbm.1, s32[12,64]{1,0:T(8,128)} %bitcast.7, bf16[64,1536]{1,0:T(8,128)(2,1)} %out_grad_hbm.1, ...), custom_call_target="tpu_custom_call" | custom-call | tf_op jit(solution)/shard_map/pallas_call | solution.py:476
  37.3 4.4 %shard_map.103 = (bf16[16,1536]{1,0:T(8,128)(2,1)}, f32[1,128]{1,0:T(1,128)}, bf16[1536,1024]{1,0:T(8,128)(2,1)}, bf16[1024,1536]{1,0:T(8,128)(2,1)}) custom-call(bf16[16,1536]{1,0:T(8,128)(2,1)} %get-tuple-element.14.token_hbm, f32[1,128]{1,0:T(1,128)} %get-tuple-element.15.gate_hbm, bf16[160,1536]{1,0:T(8,128)(2,1)} %get-tuple-element.16.rows_hbm, ...), custom_call_target="tpu_custom_call" | custom-call | tf_op jit(solution)/shard_map/pallas_call | solution.py:580

commit v3 on v2

--- a/solution.py
+++ b/solution.py
@@ -144,7 +144,9 @@
     z, x = me // 2, me % 2
     order = [(z + 2) % 4, 3 - z, z + 1 - 2 * (z % 2), z]
     partner = 2 * z + 1 - x
-    peers = [2 * g + i for g in order[:3] for i in (x, 1 - x)] + [partner]
+    far = [2 * g + i for g in order[:2] for i in (x, 1 - x)]
+    near = [2 * order[2] + i for i in (x, 1 - x)] + [partner]
+    peers = far + near
     mates = [buddy, across, diagonal]
     for d in peers:
         pl.semaphore_signal(barrier, inc=1, device_id=(d, t), device_id_type=MESH)
@@ -182,33 +184,37 @@
             extra_picks[c, span, :] = jnp.where(part_id == c, rest_hit, 0.0).astype(jnp.bfloat16)
 
     blocks = exponents.shape[0]
-    chosen = (
-        lax.broadcasted_iota(jnp.int32, (blocks, 4), 0) == 3 * t + lax.broadcasted_iota(jnp.int32, (blocks, 4), 1)
-    ).astype(jnp.bfloat16)
+    block_id = lax.broadcasted_iota(jnp.int32, (blocks, 8), 0)
+    part_no = lax.broadcasted_iota(jnp.int32, (blocks, 8), 1)
+    chosen = (block_id == jnp.where(part_no < 4, 3 * t + part_no, 3 * across + part_no - 4)).astype(jnp.bfloat16)
     loads[1].wait()
     factors = contract(jnp.exp2(exponents[...].astype(jnp.float32)).astype(jnp.bfloat16), chosen, 0, 0)
-    my_cols = pl.ds(pl.multiple_of(t * quarter, 128), quarter)
-
-    def scale(values):
+
+    def scale(values, i):
         return jnp.concatenate(
-            [values[:, c * third : (c + 1) * third] * factors[:, c : c + 1] for c in range(3)], axis=1
+            [values[:, c * third : (c + 1) * third] * factors[:, 4 * i + c : 4 * i + c + 1] for c in range(3)], axis=1
         ).astype(jnp.bfloat16)
 
-    def fill(a, mine_here):
-        outgoing[a] = message(picks[...], extra_picks[...], mine_here).reshape(experts, 16, 4 * third)
-        parts[a, t, me] = outgoing[a, me]
-
-    def send(a, d):
-        return pltpu.make_async_remote_copy(
-            src_ref=outgoing.at[a, d], dst_ref=parts.at[a, t, me],
-            send_sem=send_sem.at[a, d], recv_sem=recv_sem.at[a, me],
+    held_quarters = (t, across)
+
+    def fill(a, i):
+        q = held_quarters[i]
+        cols = pl.ds(pl.multiple_of(q * quarter, 128), quarter)
+        here = out_grad[:, cols] if a else scale(tokens[:, cols].astype(jnp.float32), i)
+        outgoing[a, i] = message(picks[...], extra_picks[...], here).reshape(experts, 16, 4 * third)
+        parts[a, q, me] = outgoing[a, i, me]
+
+    def send(a, i, d):
+        return pltpu.make_async_remote_copy(
+            src_ref=outgoing.at[a, i, d], dst_ref=parts.at[a, held_quarters[i], me],
+            send_sem=send_sem.at[a, i, d], recv_sem=recv_sem.at[a, i, me],
             device_id=(d, t), device_id_type=MESH,
         )
 
-    def arrival(a, k):
-        return pltpu.make_async_remote_copy(
-            src_ref=outgoing.at[a, k], dst_ref=parts.at[a, t, k],
-            send_sem=send_sem.at[a, k], recv_sem=recv_sem.at[a, k],
+    def arrival(a, i, k):
+        return pltpu.make_async_remote_copy(
+            src_ref=outgoing.at[a, i, k], dst_ref=parts.at[a, held_quarters[i], k],
+            send_sem=send_sem.at[a, i, k], recv_sem=recv_sem.at[a, i, k],
             device_id=(k, t), device_id_type=MESH,
         )
 
@@ -232,15 +238,16 @@
             device_id=(me, mate), device_id_type=MESH,
         )
 
-    loads[2].wait()
-    fill(0, scale(tokens[:, my_cols].astype(jnp.float32)))
-    pl.semaphore_wait(barrier, len(peers) + len(mates))
-    for d in peers:
-        send(0, d).start()
-    loads[3].wait()
-    fill(1, out_grad[:, my_cols])
-    for d in peers:
-        send(1, d).start()
+    for a in range(2):
+        loads[2 + a].wait()
+        fill(a, 0)
+        if a == 0:
+            pl.semaphore_wait(barrier, len(peers) + len(mates))
+        for d in peers:
+            send(a, 0, d).start()
+        fill(a, 1)
+        for d in near:
+            send(a, 1, d).start()
     for load in loads[5:]:
         load.start()
 
@@ -275,14 +282,20 @@
         )[i]
         return pltpu.make_async_copy(held, out, store_sem.at[i])
 
-    def take(a, g):
-        if g is order[3]:
-            arrival(a, partner).wait_recv()
-        else:
-            arrival(a, 2 * g).wait_recv()
-            arrival(a, 2 * g + 1).wait_recv()
-        passing(a, 1, g).start()
-        passing(a, 0, g).start()
+    def take_near(a):
+        for i, kind in ((0, 0), (1, 2)):
+            arrival(a, i, partner).wait_recv()
+            passing(a, kind, order[3]).start()
+            arrival(a, i, 2 * order[2]).wait_recv()
+            arrival(a, i, 2 * order[2] + 1).wait_recv()
+            passing(a, kind, order[2]).start()
+
+    def take_far(a):
+        for g in order[:2]:
+            arrival(a, 0, 2 * g).wait_recv()
+            arrival(a, 0, 2 * g + 1).wait_recv()
+            passing(a, 1, g).start()
+            passing(a, 0, g).start()
 
     def relay(a, g):
         passed(a, 1, g).wait_recv()
@@ -300,24 +313,23 @@
             target[pl.ds(lead_rows, rest_rows), some] = rest[c * rest_rows : (c + 1) * rest_rows]
         return cols
 
-    for g in near_first:
-        take(0, g)
-    for g in near_first[:2]:
-        take(1, g)
-    for g in near_first:
+    take_near(0)
+    take_far(0)
+    take_near(1)
+    for g in order[:2]:
         relay(0, g)
-    for g in near_first[2:]:
-        take(1, g)
+    take_far(1)
     for kind in (0, 2):
         for g in near_first:
             passed(0, kind, g).wait_recv()
     for q in range(tensors):
         arrange(0, q, rows)
     loads[5].wait()
-    for i, g in enumerate(near_first):
+    for i in range(groups):
         cols = pl.ds(i * hidden_block, hidden_block)
         v = jnp.dot(rows[...], w_in[:, cols], preferred_element_type=jnp.float32)
-        relay(1, g)
+        if i % 2 == 1:
+            relay(1, order[i // 2])
         square = v * v
         tanh = jnp.tanh(ROOT * (v + CUBIC * v * square))
         half = 0.5 * (1.0 + tanh)
@@ -419,10 +431,14 @@
     store(5).start()
     for a in range(2):
         for d in peers:
-            send(a, d).wait_send()
-        for kind in range(3):
-            for g in range(groups):
-                passing(a, kind, g).wait_send()
+            send(a, 0, d).wait_send()
+        for d in near:
+            send(a, 1, d).wait_send()
+        for g in order:
+            passing(a, 0, g).wait_send()
+            passing(a, 2, g).wait_send()
+        for g in order[:2]:
+            passing(a, 1, g).wait_send()
     for i in range(2):
         to_core(i).wait_send()
     for i in range(len(spans)):
@@ -434,7 +450,7 @@
     pieces = [
         sums[:, c * third : (c + 1) * third] + contract(extra_picks[c], returned, 0, 0) for c in range(3)
     ]
-    last_out[...] = scale(jnp.concatenate(pieces, axis=1)).reshape(tensors, tok_count // tensors, quarter)
+    last_out[...] = scale(jnp.concatenate(pieces, axis=1), 0).reshape(tensors, tok_count // tensors, quarter)
     last_in[t] = last_out[t]
 
     def finish(i, slot):
@@ -502,7 +518,7 @@
             pltpu.VMEM((experts * 16, tok_count), bf16),
             pltpu.VMEM((3, experts * 16, tok_count), bf16),
             pltpu.VMEM((count, slots.shape[1]), f32),
-            pltpu.VMEM((2, experts, 16, wide), bf16),
+            pltpu.VMEM((2, 2, experts, 16, wide), bf16),
             pltpu.VMEM((2, tensors, experts, 16, wide), bf16),
             pltpu.VMEM((count, width), bf16),
             pltpu.VMEM((count, hid), f32),
@@ -518,8 +534,8 @@
             pltpu.VMEM((tensors, tok_count // tensors, quarter), bf16),
             pltpu.VMEM((tensors, 8, slots.shape[1]), f32),
             dma((7,)),
-            dma((2, experts)),
-            dma((2, experts)),
+            dma((2, 2, experts)),
+            dma((2, 2, experts)),
             dma((2, 3, experts // 2)),
             dma((2, 3, experts // 2)),
             dma((2,)),

time: 41.8 us -> 42.1 us (level)
  no operation moved by 1% of the time
where the time goes in v3:
time: 42.1 us; the launch traced here: 41.9 us
  Pallas kernels  41.3 us (98%)
  between operations  0.64 us (2%)
    pallas_call x1, Pallas kernels, exchange(): pl.pallas_call(functools.partial(exchange_kernel, experts, tensors), out_...  36.9 us
    pallas_call x1, Pallas kernels, weight_grads(): pl.pallas_call(weights_kernel, out_shape=(like(token_grad), like(gate_gra...  4.35 us

profile of v3, /device:TPU:0, one launch (start us, length us, event | category | flops | bytes accessed | tf_op | source)
XLA Modules:
  0.0 41.9 jit_solution(7781138183412628318)
XLA Ops:
  0.6 36.9 %shard_map.102 = (bf16[16,1536]{1,0:T(8,128)(2,1)}, f32[1,128]{1,0:T(1,128)}, bf16[160,1536]{1,0:T(8,128)(2,1)}, bf16[160,1536]{1,0:T(8,128)(2,1)}, bf16[160,102...) custom-call(bf16[64,1536]{1,0:T(8,128)(2,1)} %tokens_hbm.1, s32[12,64]{1,0:T(8,128)} %bitcast.7, bf16[64,1536]{1,0:T(8,128)(2,1)} %out_grad_hbm.1, ...), custom_call_target="tpu_custom_call" | custom-call | tf_op jit(solution)/shard_map/pallas_call | solution.py:492
  37.6 4.3 %shard_map.103 = (bf16[16,1536]{1,0:T(8,128)(2,1)}, f32[1,128]{1,0:T(1,128)}, bf16[1536,1024]{1,0:T(8,128)(2,1)}, bf16[1024,1536]{1,0:T(8,128)(2,1)}) custom-call(bf16[16,1536]{1,0:T(8,128)(2,1)} %get-tuple-element.14.token_hbm, f32[1,128]{1,0:T(1,128)} %get-tuple-element.15.gate_hbm, bf16[160,1536]{1,0:T(8,128)(2,1)} %get-tuple-element.16.rows_hbm, ...), custom_call_target="tpu_custom_call" | custom-call | tf_op jit(solution)/shard_map/pallas_call | solution.py:596

commit v4 on v2

--- a/solution.py
+++ b/solution.py
@@ -111,7 +111,7 @@
     token_out, gate_out, rows_out, gated_out, hidden_out, dpre_out,
     token_held, gate_held, rows, gated, hidden, dpre,
     tokens, exponents, out_grad, slots, gates,
-    w_in, w_out, picks, extra_picks, place, outgoing, parts, grads, slope, upstream,
+    w_in, w_out, picks, extra_picks, place, outgoing, parts, grads, slope,
     core_out, core_in, side_out, side_in, mine, back_out, back_in, last_out, last_in, gate_parts,
     load_sem, send_sem, recv_sem, pass_send, pass_recv, ret_send, ret_recv, side_send, side_recv,
     back_send, back_recv, last_send, last_recv, gate_send, gate_recv, store_sem,
@@ -300,14 +300,11 @@
             target[pl.ds(lead_rows, rest_rows), some] = rest[c * rest_rows : (c + 1) * rest_rows]
         return cols
 
-    for g in near_first:
-        take(0, g)
-    for g in near_first[:2]:
-        take(1, g)
+    for a in range(2):
+        for g in near_first:
+            take(a, g)
     for g in near_first:
         relay(0, g)
-    for g in near_first[2:]:
-        take(1, g)
     for kind in (0, 2):
         for g in near_first:
             passed(0, kind, g).wait_recv()
@@ -328,20 +325,15 @@
     store(3).start()
 
     loads[6].wait()
-    for i, (q, kind) in enumerate(((t, None), (buddy, 0), (across, None))):
-        if kind is not None:
-            for g in near_first:
-                passed(1, kind, g).wait_recv()
-        part = arrange(1, q, grads)
-        term = contract(grads[:, part], w_out[:, part], 1, 1)
-        upstream[...] = term if i == 0 else upstream[...] + term
-    for g in near_first:
-        passed(1, 2, g).wait_recv()
-    last_part = arrange(1, diagonal, grads)
+    for kind in (0, 2):
+        for g in near_first:
+            passed(1, kind, g).wait_recv()
+    for q in range(tensors):
+        arrange(1, q, grads)
 
     def backward(i, total):
         cols = block_of(i)
-        up = upstream[:, cols] + contract(grads[:, last_part], w_out[cols, last_part], 1, 1)
+        up = contract(grads[...], w_out[cols, :], 1, 1)
         dpre[:, cols] = (gate_flat * up * slope[:, cols]).astype(jnp.bfloat16)
         return total + jnp.sum(hidden[:, cols].astype(jnp.float32) * up, axis=1, keepdims=True)
 
@@ -506,7 +498,6 @@
             pltpu.VMEM((2, tensors, experts, 16, wide), bf16),
             pltpu.VMEM((count, width), bf16),
             pltpu.VMEM((count, hid), f32),
-            pltpu.VMEM((count, hid), f32),
             pltpu.VMEM((2, count, quarter), bf16),
             pltpu.VMEM((2, count, quarter), bf16),
             pltpu.VMEM((count, quarter), bf16),

time: 41.8 us -> 41.6 us (level)
  no operation moved by 1% of the time
where the time goes in v4:
time: 41.6 us; the launch traced here: 41.5 us
  Pallas kernels  40.8 us (98%)
  between operations  0.64 us (2%)
    pallas_call x1, Pallas kernels, exchange(): pl.pallas_call(functools.partial(exchange_kernel, experts, tensors), out_...  36.5 us
    pallas_call x1, Pallas kernels, weight_grads(): pl.pallas_call(weights_kernel, out_shape=(like(token_grad), like(gate_gra...  4.35 us

profile of v4, /device:TPU:0, one launch (start us, length us, event | category | flops | bytes accessed | tf_op | source)
XLA Modules:
  0.0 41.5 jit_solution(390418183648269712)
XLA Ops:
  0.6 36.5 %shard_map.102 = (bf16[16,1536]{1,0:T(8,128)(2,1)}, f32[1,128]{1,0:T(1,128)}, bf16[160,1536]{1,0:T(8,128)(2,1)}, bf16[160,1536]{1,0:T(8,128)(2,1)}, bf16[160,102...) custom-call(bf16[64,1536]{1,0:T(8,128)(2,1)} %tokens_hbm.1, s32[12,64]{1,0:T(8,128)} %bitcast.7, bf16[64,1536]{1,0:T(8,128)(2,1)} %out_grad_hbm.1, ...), custom_call_target="tpu_custom_call" | custom-call | tf_op jit(solution)/shard_map/pallas_call | solution.py:468
  37.1 4.4 %shard_map.103 = (bf16[16,1536]{1,0:T(8,128)(2,1)}, f32[1,128]{1,0:T(1,128)}, bf16[1536,1024]{1,0:T(8,128)(2,1)}, bf16[1024,1536]{1,0:T(8,128)(2,1)}) custom-call(bf16[16,1536]{1,0:T(8,128)(2,1)} %get-tuple-element.14.token_hbm, f32[1,128]{1,0:T(1,128)} %get-tuple-element.15.gate_hbm, bf16[160,1536]{1,0:T(8,128)(2,1)} %get-tuple-element.16.rows_hbm, ...), custom_call_target="tpu_custom_call" | custom-call | tf_op jit(solution)/shard_map/pallas_call | solution.py:571
